TPU v7x, 256 devices: a whole 4x4x8 slice. The times are simulated.
256 devices in a mesh: row: 16 (over z, core), col: 8 (over y_hi, x), rep: 2 (over y_lo).
Axes of the slice: x: 4, y: 4 (y_hi: 2, y_lo: 2; y = y_hi * 2 + y_lo), z: 8, core: 2. Of those that a mesh axis runs over, the one named last changes fastest.
Arguments:
- node_features: bfloat16 [65536, 256], P(('row', 'col', 'rep')), may hold values from -6 to 6
- weight: bfloat16 [256, 256], replicated, may hold values from -0.375 to 0.375
- cotangent: bfloat16 [65536, 256], P(('col', 'rep', 'row')), may hold values from -6 to 6
- adjacency_blocks: bfloat16 [16, 16, 256, 128, 128], P(('col', 'rep'), 'row'), may hold values from -0.0625 to 0.0625
- block_coords: int32 [16, 16, 2, 256], P(('col', 'rep'), 'row'), may hold values from 0 to 31, as said below
- block_counts: int32 [16, 16], P(('col', 'rep'), 'row'), may hold values from 1 to 256, as said below
Outputs:
- hidden: bfloat16 [65536, 256], P(('col', 'rep', 'row'))
- weight_grad: float32 [256, 256], replicated
- feature_grad: bfloat16 [65536, 256], P(('row', 'col', 'rep'))
Inputs may be any that keep to these rules, and one draw needn't show every extreme that they name: block_coords[i, r, 0, k] is a block row below 32 and block_coords[i, r, 1, k] a block column below 32; within a tile the first min(256, 1024) slots name distinct positions. Only the first block_counts[i, r] slots of tile (i, r) belong to the adjacency; the values and coordinates in its other slots are not part of it.
All inputs are finite; a program needn't handle non-finite values.
Results may differ from a plain program's by a relative error of at most 0.029.
Values may be sent and summed in bfloat16 or wider, within the bound.
No kernel may reach another device: no remote copies, remote signals or barrier semaphores. Data moves between devices by JAX's collectives and lax.ppermute only.
A program may use at most 128 MiB of HBM per device.

v0:
```python
import math
import jax
import jax.numpy as jnp
from jax import lax
from jax.sharding import PartitionSpec as P


def silu_slope(values):
    sigma = jax.nn.sigmoid(values)
    return sigma * (1.0 + values * (1.0 - sigma))


def tile_product(blocks, coords, filled, source, out_blocks, flipped):
    slot_total = blocks.shape[0]
    block_size = blocks.shape[1]
    feature_width = source.shape[1]
    group_size = math.gcd(slot_total, 64)
    groups = slot_total // group_size
    source_blocks = source.reshape(-1, block_size, feature_width)
    take_index = coords[0] if flipped else coords[1]
    put_index = coords[1] if flipped else coords[0]
    active = (jnp.arange(slot_total, dtype=jnp.int32) < filled).astype(jnp.float32)
    einsum_form = "kba,kbf->kaf" if flipped else "kab,kbf->kaf"
    targets = jnp.arange(out_blocks, dtype=jnp.int32)

    def accumulate(running, pieces):
        block_group, take_group, put_group, active_group = pieces
        gathered = source_blocks[take_group]
        product = jnp.einsum(einsum_form, block_group, gathered, preferred_element_type=jnp.float32)
        placing = (put_group[:, None] == targets[None, :]).astype(jnp.float32) * active_group[
            :, None
        ]
        flat = product.reshape(group_size, block_size * feature_width)
        placed = lax.dot_general(
            placing,
            flat,
            (((0,), (0,)), ((), ())),
            precision=lax.Precision.HIGHEST,
            preferred_element_type=jnp.float32,
        )
        return (running + placed, None)

    running = jnp.zeros((out_blocks, block_size * feature_width), jnp.float32)
    running, _ = lax.scan(
        accumulate,
        running,
        (
            blocks.reshape(groups, group_size, block_size, block_size),
            take_index.reshape(groups, group_size),
            put_index.reshape(groups, group_size),
            active.reshape(groups, group_size),
        ),
    )
    return running.reshape(out_blocks * block_size, feature_width)


def body(node_features, weight, cotangent, adjacency_blocks, block_coords, block_counts):
    blocks = adjacency_blocks[0, 0]
    coords = block_coords[0, 0]
    filled = block_counts[0, 0]
    block_size = blocks.shape[-1]
    local_nodes = node_features.shape[0]
    row_devices = lax.axis_size("row")
    node_total = local_nodes * row_devices * lax.axis_size("col") * lax.axis_size("rep")
    tile_rows = local_nodes * row_devices
    column_feats = lax.all_gather(node_features, ("col", "rep"), axis=0, tiled=True)
    tile_cols = column_feats.shape[0]
    partial_value = tile_product(
        blocks, coords, filled, column_feats, tile_rows // block_size, False
    )
    own_sum = lax.psum_scatter(
        partial_value.astype(jnp.bfloat16), "row", scatter_dimension=0, tiled=True
    )
    pre_act = jnp.dot(own_sum, weight, preferred_element_type=jnp.float32)
    hidden = jax.nn.silu(pre_act).astype(jnp.bfloat16)
    own_grad = (cotangent.astype(jnp.float32) * silu_slope(pre_act)).astype(jnp.bfloat16)
    own_mixed_grad = jnp.dot(own_grad, weight.T, preferred_element_type=jnp.float32).astype(
        jnp.bfloat16
    )
    panel_grad = lax.all_gather(own_mixed_grad, "row", axis=0, tiled=True)
    weight_part = lax.dot_general(
        own_sum, own_grad, (((0,), (0,)), ((), ())), preferred_element_type=jnp.float32
    )
    weight_grad = lax.psum(weight_part, ("row", "col", "rep")) / math.sqrt(node_total)
    back_terms = tile_product(blocks, coords, filled, panel_grad, tile_cols // block_size, True)
    feature_grad = lax.psum_scatter(
        back_terms.astype(jnp.bfloat16), ("col", "rep"), scatter_dimension=0, tiled=True
    )
    return (hidden, weight_grad, feature_grad)


def solution(mesh):
    in_specs = (
        P(("row", "col", "rep"), None),
        P(),
        P(("col", "rep", "row"), None),
        P(("col", "rep"), "row", None, None, None),
        P(("col", "rep"), "row", None, None),
        P(("col", "rep"), "row"),
    )
    out_specs = (P(("col", "rep", "row"), None), P(), P(("row", "col", "rep"), None))
    return jax.shard_map(body, mesh=mesh, in_specs=in_specs, out_specs=out_specs, check_vma=False)
```

profile of v0, /device:TPU:32, one launch (start us, length us, event | category | flops | bytes accessed | tf_op | source)
XLA Modules:
  0.0 642.4 jit_solution(17018396184696318942)
XLA Ops:
  9.6 81.7 %all-gather.3.cloned.1.call-done = bf16[4096,256]{1,0:T(8,128)(2,1)} async-done(((bf16[256,256]{1,0:T(8,128)(2,1)}), bf16[4096,256]{1,0:T(8,128)(2,1)}) %all-gather.3.cloned.1.call-update) | async-done | bytes 2097168 | tf_op jit(solution)/shard_map/all_gather | solution.py:66
  91.3 99.7 %while.22 = (s32[]{:T(128)}, f32[32,32768]{1,0:T(8,128)}, s32[4,64]{1,0:T(4,128)S(1)}, f32[4,64]{1,0:T(4,128)S(1)}, bf16[4,64,128,128]{3,2,1,0:T(8,128)(2,1)}, /...) while((s32[]{:T(128)}, f32[32,32768]{1,0:T(8,128)}, ...), condition=%wide.region_1.2_spmd.clone, body=%wide.region_0.1_spmd.clone.sunk | while | flops 1344279808 | bytes 56630384 | solution.py:44
  99.7 8.0 %copy.16 = f32[8,8,128,256]{3,1,2,0:T(8,128)} copy(f32[8,8,128,256]{3,2,1,0:T(8,128)S(1)} %bitcast.88) | data formatting | bytes 16777216 | tf_op jit(solution)/shard_map/while
  107.7 8.0 %convolution_add_fusion.4 = f32[32,32768]{1,0:T(8,128)} fusion(f32[64,32768]{1,0:T(8,128)} %bitcast.86, f32[32,32768]{1,0:T(8,128)} %get-tuple-element.276, pred[]{:T(512)S(6)} %compare.6, f32[64]{0:T(128)S(1)} %fusion.64, s32[64]{0:T(128)S(1)} %fusion.65), kind=kOutput, calls=%fused_computation.4.clone.1 | convolution fusion | flops 807407616 | bytes 16777728 | tf_op jit(solution)/shard_map/while/body/eval_jaxpr/dot_general | solution.py:34
  124.1 8.0 %copy.16 = f32[8,8,128,256]{3,1,2,0:T(8,128)} copy(f32[8,8,128,256]{3,2,1,0:T(8,128)S(1)} %bitcast.88) | data formatting | bytes 16777216 | tf_op jit(solution)/shard_map/while
  132.1 8.7 %convolution_add_fusion.4 = f32[32,32768]{1,0:T(8,128)} fusion(f32[64,32768]{1,0:T(8,128)} %bitcast.86, f32[32,32768]{1,0:T(8,128)} %get-tuple-element.276, pred[]{:T(512)S(6)} %compare.6, f32[64]{0:T(128)S(1)} %fusion.64, s32[64]{0:T(128)S(1)} %fusion.65), kind=kOutput, calls=%fused_computation.4.clone.1 | convolution fusion | flops 807407616 | bytes 16777728 | tf_op jit(solution)/shard_map/while/body/eval_jaxpr/dot_general | solution.py:34
  149.2 8.0 %copy.16 = f32[8,8,128,256]{3,1,2,0:T(8,128)} copy(f32[8,8,128,256]{3,2,1,0:T(8,128)S(1)} %bitcast.88) | data formatting | bytes 16777216 | tf_op jit(solution)/shard_map/while
  157.2 8.7 %convolution_add_fusion.4 = f32[32,32768]{1,0:T(8,128)} fusion(f32[64,32768]{1,0:T(8,128)} %bitcast.86, f32[32,32768]{1,0:T(8,128)} %get-tuple-element.276, pred[]{:T(512)S(6)} %compare.6, f32[64]{0:T(128)S(1)} %fusion.64, s32[64]{0:T(128)S(1)} %fusion.65), kind=kOutput, calls=%fused_computation.4.clone.1 | convolution fusion | flops 807407616 | bytes 16777728 | tf_op jit(solution)/shard_map/while/body/eval_jaxpr/dot_general | solution.py:34
  174.3 8.0 %copy.16 = f32[8,8,128,256]{3,1,2,0:T(8,128)} copy(f32[8,8,128,256]{3,2,1,0:T(8,128)S(1)} %bitcast.88) | data formatting | bytes 16777216 | tf_op jit(solution)/shard_map/while
  182.3 8.7 %convolution_add_fusion.4 = f32[32,32768]{1,0:T(8,128)} fusion(f32[64,32768]{1,0:T(8,128)} %bitcast.86, f32[32,32768]{1,0:T(8,128)} %get-tuple-element.276, pred[]{:T(512)S(6)} %compare.6, f32[64]{0:T(128)S(1)} %fusion.64, s32[64]{0:T(128)S(1)} %fusion.65), kind=kOutput, calls=%fused_computation.4.clone.1 | convolution fusion | flops 807407616 | bytes 16777728 | tf_op jit(solution)/shard_map/while/body/eval_jaxpr/dot_general | solution.py:34
  195.8 56.5 %reduce-scatter.3.cloned.1.call-done = bf16[256,256]{1,0:T(8,128)(2,1)} async-done(((bf16[4096,256]{1,0:T(8,128)(2,1)}), bf16[256,256]{1,0:T(8,128)(2,1)}) %reduce-scatter.3.cloned.1.call-update) | async-done | bytes 131088 | tf_op jit(solution)/shard_map/reduce_scatter | solution.py:71
  255.1 12.0 %copy.9 = bf16[1,1,256,128,128]{3,4,2,1,0:T(8,128)(2,1)} copy(bf16[1,1,256,128,128]{4,3,2,1,0:T(8,128)(2,1)} %bitcast.93) | data formatting | bytes 16777216 | tf_op args[3]
  268.3 27.7 %all-gather.5.cloned.1.call-done = bf16[4096,256]{1,0:T(8,128)(2,1)} async-done(((bf16[256,256]{1,0:T(8,128)(2,1)}), bf16[4096,256]{1,0:T(8,128)(2,1)}) %all-gather.5.cloned.1.call-update) | async-done | bytes 2097168 | tf_op jit(solution)/shard_map/all_gather | solution.py:80
  296.0 99.8 %while.23 = (s32[]{:T(128)}, f32[32,32768]{1,0:T(8,128)}, s32[4,64]{1,0:T(4,128)S(1)}, f32[4,64]{1,0:T(4,128)S(1)}, bf16[4,64,128,128]{2,3,1,0:T(8,128)(2,1)}, /...) while((s32[]{:T(128)}, f32[32,32768]{1,0:T(8,128)}, ...), condition=%wide.region_5.6_spmd.clone, body=%wide.region_4.5_spmd.clone.sunk | while | flops 1344279808 | bytes 56630384 | solution.py:44
  304.5 8.0 %copy.17 = f32[8,8,128,256]{3,1,2,0:T(8,128)} copy(f32[8,8,128,256]{3,2,1,0:T(8,128)S(1)} %bitcast.89) | data formatting | bytes 16777216 | tf_op jit(solution)/shard_map/while
  312.4 8.0 %convolution_add_fusion.5 = f32[32,32768]{1,0:T(8,128)} fusion(f32[64,32768]{1,0:T(8,128)} %bitcast.87, f32[32,32768]{1,0:T(8,128)} %get-tuple-element.303, pred[]{:T(512)S(6)} %compare.7, f32[64]{0:T(128)S(1)} %fusion.72, s32[64]{0:T(128)S(1)} %fusion.73), kind=kOutput, calls=%fused_computation.24.clone.1 | convolution fusion | flops 807407616 | bytes 16777728 | tf_op jit(solution)/shard_map/while/body/eval_jaxpr/dot_general | solution.py:34
  328.9 8.0 %copy.17 = f32[8,8,128,256]{3,1,2,0:T(8,128)} copy(f32[8,8,128,256]{3,2,1,0:T(8,128)S(1)} %bitcast.89) | data formatting | bytes 16777216 | tf_op jit(solution)/shard_map/while
  336.9 8.7 %convolution_add_fusion.5 = f32[32,32768]{1,0:T(8,128)} fusion(f32[64,32768]{1,0:T(8,128)} %bitcast.87, f32[32,32768]{1,0:T(8,128)} %get-tuple-element.303, pred[]{:T(512)S(6)} %compare.7, f32[64]{0:T(128)S(1)} %fusion.72, s32[64]{0:T(128)S(1)} %fusion.73), kind=kOutput, calls=%fused_computation.24.clone.1 | convolution fusion | flops 807407616 | bytes 16777728 | tf_op jit(solution)/shard_map/while/body/eval_jaxpr/dot_general | solution.py:34
  354.1 8.0 %copy.17 = f32[8,8,128,256]{3,1,2,0:T(8,128)} copy(f32[8,8,128,256]{3,2,1,0:T(8,128)S(1)} %bitcast.89) | data formatting | bytes 16777216 | tf_op jit(solution)/shard_map/while
  362.0 8.6 %convolution_add_fusion.5 = f32[32,32768]{1,0:T(8,128)} fusion(f32[64,32768]{1,0:T(8,128)} %bitcast.87, f32[32,32768]{1,0:T(8,128)} %get-tuple-element.303, pred[]{:T(512)S(6)} %compare.7, f32[64]{0:T(128)S(1)} %fusion.72, s32[64]{0:T(128)S(1)} %fusion.73), kind=kOutput, calls=%fused_computation.24.clone.1 | convolution fusion | flops 807407616 | bytes 16777728 | tf_op jit(solution)/shard_map/while/body/eval_jaxpr/dot_general | solution.py:34
  379.2 8.0 %copy.17 = f32[8,8,128,256]{3,1,2,0:T(8,128)} copy(f32[8,8,128,256]{3,2,1,0:T(8,128)S(1)} %bitcast.89) | data formatting | bytes 16777216 | tf_op jit(solution)/shard_map/while
  387.1 8.7 %convolution_add_fusion.5 = f32[32,32768]{1,0:T(8,128)} fusion(f32[64,32768]{1,0:T(8,128)} %bitcast.87, f32[32,32768]{1,0:T(8,128)} %get-tuple-element.303, pred[]{:T(512)S(6)} %compare.7, f32[64]{0:T(128)S(1)} %fusion.72, s32[64]{0:T(128)S(1)} %fusion.73), kind=kOutput, calls=%fused_computation.24.clone.1 | convolution fusion | flops 807407616 | bytes 16777728 | tf_op jit(solution)/shard_map/while/body/eval_jaxpr/dot_general | solution.py:34
  400.6 148.2 %all-reduce.2.cloned.1.call-done = f32[256,256]{1,0:T(8,128)} async-done(((f32[256,256]{1,0:T(8,128)}), f32[256,256]{1,0:T(8,128)}) %all-reduce.2.cloned.1.call-update) | async-done | bytes 262160 | tf_op jit(solution)/shard_map/psum | solution.py:84
  550.5 85.3 %reduce-scatter.5.cloned.1.call-done = bf16[256,256]{1,0:T(8,128)(2,1)} async-done(((bf16[4096,256]{1,0:T(8,128)(2,1)}), bf16[256,256]{1,0:T(8,128)(2,1)}) %reduce-scatter.5.cloned.1.call-update) | async-done | bytes 131088 | tf_op jit(solution)/shard_map/reduce_scatter | solution.py:86
  (80 shorter events, 84.5 us)
Async XLA Ops:
  7.2 245.1 %copy-start = (bf16[256,256]{1,0:T(8,128)(2,1)S(1)}, bf16[256,256]{1,0:T(8,128)(2,1)}, u32[]{:S(2)}) copy-start(bf16[256,256]{1,0:T(8,128)(2,1)} %param.11) | copy-start | bytes 393220
  7.2 84.1 %all-gather.3.cloned.1.call-start = ((), (), s32[]{:S(2)}) async-start(), calls=%async_computation.2 | async-start | bytes 2228224 | tf_op jit(solution)/shard_map/all_gather | solution.py:66
  7.9 244.4 %reduce-scatter.3.cloned.1.call-start = ((), (), s32[]{:S(2)}) async-start(), calls=%async_computation.3 | async-start | bytes 2228224 | tf_op jit(solution)/shard_map/reduce_scatter | solution.py:71
  193.4 58.9 %copy-start.3 = (bf16[256,256]{1,0:T(8,128)(2,1)S(1)}, bf16[256,256]{1,0:T(8,128)(2,1)}, u32[]{:S(2)}) copy-start(bf16[256,256]{1,0:T(8,128)(2,1)} %param.12) | copy-start | bytes 393220
  195.8 100.3 %all-gather.5.cloned.1.call-start = ((), (), s32[]{:S(2)}) async-start(), calls=%async_computation.5 | async-start | bytes 2228224 | tf_op jit(solution)/shard_map/all_gather | solution.py:80
  255.0 12.1 %copy-start.2 = (bf16[256,256]{1,0:T(8,128)(2,1)S(1)}, bf16[256,256]{1,0:T(8,128)(2,1)}, u32[]{:S(2)}) copy-start(bf16[256,256]{1,0:T(8,128)(2,1)} %reduce-scatter.3.cloned.1.call-done) | copy-start | bytes 393220
  255.0 293.8 %all-reduce.2.cloned.1.call-start = ((), (), s32[]{:S(2)}) async-start(), calls=%async_computation.4 | async-start | bytes 524288 | tf_op jit(solution)/shard_map/psum | solution.py:84
  268.1 367.8 %reduce-scatter.5.cloned.1.call-start = ((), (), s32[]{:S(2)}) async-start(), calls=%async_computation.6 | async-start | bytes 2228224 | tf_op jit(solution)/shard_map/reduce_scatter | solution.py:86
  395.8 240.0 %copy-start.1 = (bf16[256,256]{1,0:T(8,128)(2,1)S(1)}, bf16[256,256]{1,0:T(8,128)(2,1)}, u32[]{:S(2)}) copy-start(bf16[256,256]{1,0:T(8,128)(2,1)} %param.11) | copy-start | bytes 393220
Sparse Core Ops, SparseCore 0:
  9.8 81.4 all-gather.2
  195.9 56.3 reduce-scatter.2
  255.2 40.8 all-gather.4
  301.9 246.9 all-reduce.1
  551.8 83.9 reduce-scatter.4
where the time goes:
time: 643 us; the launch traced here: 642 us
  waiting for transfers between devices  400 us (62%)
  local copies, waits for them, and re-layouts  116 us (18%)
  matrix products  104 us (16%)
  between operations  14.5 us (2%)
  other arithmetic  6.61 us (1%)
    psum x1, waiting for transfers between devices, body(): lax.psum(weight_part, ('row', 'col', 'rep')) / math.sqrt(node_total)  148 us
    reduce_scatter x1, waiting for transfers between devices, body(): lax.psum_scatter(back_terms.astype(jnp.bfloat16), ('col', 'rep'), scatter...  85.3 us
    all_gather x1, waiting for transfers between devices, body(): lax.all_gather(node_features, ('col', 'rep'), axis=0, tiled=True)  81.7 us
    dot_general x8, matrix products, accumulate(): lax.dot_general(placing, flat, (((0,), (0,)), ((), ())), precision=lax.Pr...  68 us
    while x8, local copies, waits for them, and re-layouts  63.7 us
    reduce_scatter x1, waiting for transfers between devices, body(): lax.psum_scatter(partial_value.astype(jnp.bfloat16), 'row', scatter_dimen...  56.5 us
    gather x8, local copies, waits for them, and re-layouts, accumulate(): gathered = source_blocks[take_group]  34.8 us
    dot_general x8, matrix products, accumulate(): jnp.einsum(einsum_form, block_group, gathered, preferred_element_type=jnp...  32.6 us
  transfers between devices with their start and end apart: 5, of which 5 were waited for; matrix products, arithmetic and copies ran while one was open for 19% of the time, Pallas kernels for 0%

commit v1 on v0

--- a/solution.py
+++ b/solution.py
@@ -63,7 +63,12 @@
     row_devices = lax.axis_size("row")
     node_total = local_nodes * row_devices * lax.axis_size("col") * lax.axis_size("rep")
     tile_rows = local_nodes * row_devices
-    column_feats = lax.all_gather(node_features, ("col", "rep"), axis=0, tiled=True)
+    column_feats = jnp.concatenate(
+        lax.all_to_all(
+            jnp.stack([node_features] * lax.axis_size(("col", "rep"))), ("col", "rep"), 0, 0
+        ),
+        axis=0,
+    )
     tile_cols = column_feats.shape[0]
     partial_value = tile_product(
         blocks, coords, filled, column_feats, tile_rows // block_size, False

time: 643 us -> 591 us (0.919)
  waiting for transfers between devices: 400 us -> 346 us
  starting transfers between devices: 0.38 us -> 7.38 us
    all_gather x1 -> x0, waiting for transfers between devices: 81.7 us -> none  [body(): lax.all_gather(node_features, ('col', 'rep'), axis=0, tiled=True)]
    all_to_all x0 -> x1, waiting for transfers between devices: none -> 30.2 us  [body(): lax.all_to_all(jnp.stack([node_features] * lax.axis_size(('col', 'rep')))...]
    all_to_all x0 -> x1, starting transfers between devices: none -> 7.03 us  [body(): lax.all_to_all(jnp.stack([node_features] * lax.axis_size(('col', 'rep')))...]
  transfers between devices with their start and end apart: 5 -> 5, of which waited for: 5 -> 5; matrix products, arithmetic and copies ran while one was open for 19% -> 20% of each run, Pallas kernels for 0% -> 0%
where the time goes in v1:
time: 591 us
  waiting for transfers between devices  346 us (59%)
  local copies, waits for them, and re-layouts  112 us (19%)
  matrix products  104 us (18%)
  between operations  14.5 us (2%)
  starting transfers between devices  7.38 us (1%)
  other arithmetic  6.61 us (1%)
    psum x1, waiting for transfers between devices, body(): lax.psum(weight_part, ('row', 'col', 'rep')) / math.sqrt(node_total)  149 us
    reduce_scatter x1, waiting for transfers between devices, body(): lax.psum_scatter(back_terms.astype(jnp.bfloat16), ('col', 'rep'), scatter...  85.3 us
    dot_general x8, matrix products, accumulate(): lax.dot_general(placing, flat, (((0,), (0,)), ((), ())), precision=lax.Pr...  68 us
    while x8, local copies, waits for them, and re-layouts  63.7 us
    reduce_scatter x1, waiting for transfers between devices, body(): lax.psum_scatter(partial_value.astype(jnp.bfloat16), 'row', scatter_dimen...  54.4 us
    dot_general x8, matrix products, accumulate(): jnp.einsum(einsum_form, block_group, gathered, preferred_element_type=jnp...  32.5 us
    all_to_all x1, waiting for transfers between devices, body(): lax.all_to_all(jnp.stack([node_features] * lax.axis_size(('col', 'rep')))...  30.2 us
    gather x8, local copies, waits for them, and re-layouts, accumulate(): gathered = source_blocks[take_group]  28.5 us
  transfers between devices with their start and end apart: 5, of which 5 were waited for; matrix products, arithmetic and copies ran while one was open for 20% of the time, Pallas kernels for 0%

profile of v1, /device:TPU:32, one launch (start us, length us, event | category | flops | bytes accessed | tf_op | source)
XLA Modules:
  0.0 590.6 jit_solution(1414005611268056460)
XLA Ops:
  17.6 30.2 %all-to-all-done = bf16[16,256,256]{2,1,0:T(8,128)(2,1)S(1)} async-done(((bf16[16,256,256]{2,1,0:T(8,128)(2,1)}), bf16[16,256,256]{2,1,0:T(8,128)(2,1)S(1)}, u32[]{:S(2)}, u32[]{:S(2)}) %all-to-all-start) | async-done | bytes 2097184 | tf_op jit(solution)/shard_map/all_to_all | solution.py:67
  47.9 93.3 %while.22 = (s32[]{:T(128)}, f32[32,32768]{1,0:T(8,128)}, s32[4,64]{1,0:T(4,128)S(1)}, f32[4,64]{1,0:T(4,128)S(1)}, bf16[4,64,128,128]{3,2,1,0:T(8,128)(2,1)}, /...) while((s32[]{:T(128)}, f32[32,32768]{1,0:T(8,128)}, ...), condition=%wide.region_1.2_spmd.clone, body=%wide.region_0.1_spmd.clone.sunk | while | flops 1344279808 | bytes 56630384 | solution.py:44
  54.7 8.0 %copy.16 = f32[8,8,128,256]{3,1,2,0:T(8,128)} copy(f32[8,8,128,256]{3,2,1,0:T(8,128)S(1)} %bitcast.88) | data formatting | bytes 16777216 | tf_op jit(solution)/shard_map/while
  62.7 8.0 %convolution_add_fusion.4 = f32[32,32768]{1,0:T(8,128)} fusion(f32[64,32768]{1,0:T(8,128)} %bitcast.86, f32[32,32768]{1,0:T(8,128)} %get-tuple-element.276, pred[]{:T(512)S(6)} %compare.6, f32[64]{0:T(128)S(1)} %fusion.64, s32[64]{0:T(128)S(1)} %fusion.65), kind=kOutput, calls=%fused_computation.4.clone.1 | convolution fusion | flops 807407616 | bytes 16777728 | tf_op jit(solution)/shard_map/while/body/eval_jaxpr/dot_general | solution.py:34
  77.5 8.0 %copy.16 = f32[8,8,128,256]{3,1,2,0:T(8,128)} copy(f32[8,8,128,256]{3,2,1,0:T(8,128)S(1)} %bitcast.88) | data formatting | bytes 16777216 | tf_op jit(solution)/shard_map/while
  85.5 8.7 %convolution_add_fusion.4 = f32[32,32768]{1,0:T(8,128)} fusion(f32[64,32768]{1,0:T(8,128)} %bitcast.86, f32[32,32768]{1,0:T(8,128)} %get-tuple-element.276, pred[]{:T(512)S(6)} %compare.6, f32[64]{0:T(128)S(1)} %fusion.64, s32[64]{0:T(128)S(1)} %fusion.65), kind=kOutput, calls=%fused_computation.4.clone.1 | convolution fusion | flops 807407616 | bytes 16777728 | tf_op jit(solution)/shard_map/while/body/eval_jaxpr/dot_general | solution.py:34
  101.0 8.0 %copy.16 = f32[8,8,128,256]{3,1,2,0:T(8,128)} copy(f32[8,8,128,256]{3,2,1,0:T(8,128)S(1)} %bitcast.88) | data formatting | bytes 16777216 | tf_op jit(solution)/shard_map/while
  109.0 8.7 %convolution_add_fusion.4 = f32[32,32768]{1,0:T(8,128)} fusion(f32[64,32768]{1,0:T(8,128)} %bitcast.86, f32[32,32768]{1,0:T(8,128)} %get-tuple-element.276, pred[]{:T(512)S(6)} %compare.6, f32[64]{0:T(128)S(1)} %fusion.64, s32[64]{0:T(128)S(1)} %fusion.65), kind=kOutput, calls=%fused_computation.4.clone.1 | convolution fusion | flops 807407616 | bytes 16777728 | tf_op jit(solution)/shard_map/while/body/eval_jaxpr/dot_general | solution.py:34
  124.5 8.0 %copy.16 = f32[8,8,128,256]{3,1,2,0:T(8,128)} copy(f32[8,8,128,256]{3,2,1,0:T(8,128)S(1)} %bitcast.88) | data formatting | bytes 16777216 | tf_op jit(solution)/shard_map/while
  132.5 8.7 %convolution_add_fusion.4 = f32[32,32768]{1,0:T(8,128)} fusion(f32[64,32768]{1,0:T(8,128)} %bitcast.86, f32[32,32768]{1,0:T(8,128)} %get-tuple-element.276, pred[]{:T(512)S(6)} %compare.6, f32[64]{0:T(128)S(1)} %fusion.64, s32[64]{0:T(128)S(1)} %fusion.65), kind=kOutput, calls=%fused_computation.4.clone.1 | convolution fusion | flops 807407616 | bytes 16777728 | tf_op jit(solution)/shard_map/while/body/eval_jaxpr/dot_general | solution.py:34
  146.0 54.4 %reduce-scatter.3.cloned.1.call-done = bf16[256,256]{1,0:T(8,128)(2,1)} async-done(((bf16[4096,256]{1,0:T(8,128)(2,1)}), bf16[256,256]{1,0:T(8,128)(2,1)}) %reduce-scatter.3.cloned.1.call-update) | async-done | bytes 131088 | tf_op jit(solution)/shard_map/reduce_scatter | solution.py:76
  203.2 12.0 %copy.9 = bf16[1,1,256,128,128]{3,4,2,1,0:T(8,128)(2,1)} copy(bf16[1,1,256,128,128]{4,3,2,1,0:T(8,128)(2,1)} %bitcast.93) | data formatting | bytes 16777216 | tf_op args[3]
  216.4 27.5 %all-gather.2.cloned.1.call-done = bf16[4096,256]{1,0:T(8,128)(2,1)} async-done(((bf16[256,256]{1,0:T(8,128)(2,1)}), bf16[4096,256]{1,0:T(8,128)(2,1)}) %all-gather.2.cloned.1.call-update) | async-done | bytes 2097168 | tf_op jit(solution)/shard_map/all_gather | solution.py:85
  243.9 99.8 %while.23 = (s32[]{:T(128)}, f32[32,32768]{1,0:T(8,128)}, s32[4,64]{1,0:T(4,128)S(1)}, f32[4,64]{1,0:T(4,128)S(1)}, bf16[4,64,128,128]{2,3,1,0:T(8,128)(2,1)}, /...) while((s32[]{:T(128)}, f32[32,32768]{1,0:T(8,128)}, ...), condition=%wide.region_5.6_spmd.clone, body=%wide.region_4.5_spmd.clone.sunk | while | flops 1344279808 | bytes 56630384 | solution.py:44
  252.4 8.0 %copy.17 = f32[8,8,128,256]{3,1,2,0:T(8,128)} copy(f32[8,8,128,256]{3,2,1,0:T(8,128)S(1)} %bitcast.89) | data formatting | bytes 16777216 | tf_op jit(solution)/shard_map/while
  260.3 8.0 %convolution_add_fusion.5 = f32[32,32768]{1,0:T(8,128)} fusion(f32[64,32768]{1,0:T(8,128)} %bitcast.87, f32[32,32768]{1,0:T(8,128)} %get-tuple-element.303, pred[]{:T(512)S(6)} %compare.7, f32[64]{0:T(128)S(1)} %fusion.72, s32[64]{0:T(128)S(1)} %fusion.73), kind=kOutput, calls=%fused_computation.24.clone.1 | convolution fusion | flops 807407616 | bytes 16777728 | tf_op jit(solution)/shard_map/while/body/eval_jaxpr/dot_general | solution.py:34
  276.8 8.0 %copy.17 = f32[8,8,128,256]{3,1,2,0:T(8,128)} copy(f32[8,8,128,256]{3,2,1,0:T(8,128)S(1)} %bitcast.89) | data formatting | bytes 16777216 | tf_op jit(solution)/shard_map/while
  284.8 8.7 %convolution_add_fusion.5 = f32[32,32768]{1,0:T(8,128)} fusion(f32[64,32768]{1,0:T(8,128)} %bitcast.87, f32[32,32768]{1,0:T(8,128)} %get-tuple-element.303, pred[]{:T(512)S(6)} %compare.7, f32[64]{0:T(128)S(1)} %fusion.72, s32[64]{0:T(128)S(1)} %fusion.73), kind=kOutput, calls=%fused_computation.24.clone.1 | convolution fusion | flops 807407616 | bytes 16777728 | tf_op jit(solution)/shard_map/while/body/eval_jaxpr/dot_general | solution.py:34
  301.9 8.0 %copy.17 = f32[8,8,128,256]{3,1,2,0:T(8,128)} copy(f32[8,8,128,256]{3,2,1,0:T(8,128)S(1)} %bitcast.89) | data formatting | bytes 16777216 | tf_op jit(solution)/shard_map/while
  309.9 8.6 %convolution_add_fusion.5 = f32[32,32768]{1,0:T(8,128)} fusion(f32[64,32768]{1,0:T(8,128)} %bitcast.87, f32[32,32768]{1,0:T(8,128)} %get-tuple-element.303, pred[]{:T(512)S(6)} %compare.7, f32[64]{0:T(128)S(1)} %fusion.72, s32[64]{0:T(128)S(1)} %fusion.73), kind=kOutput, calls=%fused_computation.24.clone.1 | convolution fusion | flops 807407616 | bytes 16777728 | tf_op jit(solution)/shard_map/while/body/eval_jaxpr/dot_general | solution.py:34
  327.0 8.0 %copy.17 = f32[8,8,128,256]{3,1,2,0:T(8,128)} copy(f32[8,8,128,256]{3,2,1,0:T(8,128)S(1)} %bitcast.89) | data formatting | bytes 16777216 | tf_op jit(solution)/shard_map/while
  335.0 8.7 %convolution_add_fusion.5 = f32[32,32768]{1,0:T(8,128)} fusion(f32[64,32768]{1,0:T(8,128)} %bitcast.87, f32[32,32768]{1,0:T(8,128)} %get-tuple-element.303, pred[]{:T(512)S(6)} %compare.7, f32[64]{0:T(128)S(1)} %fusion.72, s32[64]{0:T(128)S(1)} %fusion.73), kind=kOutput, calls=%fused_computation.24.clone.1 | convolution fusion | flops 807407616 | bytes 16777728 | tf_op jit(solution)/shard_map/while/body/eval_jaxpr/dot_general | solution.py:34
  348.5 148.6 %all-reduce.2.cloned.1.call-done = f32[256,256]{1,0:T(8,128)} async-done(((f32[256,256]{1,0:T(8,128)}), f32[256,256]{1,0:T(8,128)}) %all-reduce.2.cloned.1.call-update) | async-done | bytes 262160 | tf_op jit(solution)/shard_map/psum | solution.py:89
  498.8 85.3 %reduce-scatter.5.cloned.1.call-done = bf16[256,256]{1,0:T(8,128)(2,1)} async-done(((bf16[4096,256]{1,0:T(8,128)(2,1)}), bf16[256,256]{1,0:T(8,128)(2,1)}) %reduce-scatter.5.cloned.1.call-update) | async-done | bytes 131088 | tf_op jit(solution)/shard_map/reduce_scatter | solution.py:91
  (82 shorter events, 86.2 us)
Async XLA Ops:
  7.2 193.2 %copy-start = (bf16[256,256]{1,0:T(8,128)(2,1)S(1)}, bf16[256,256]{1,0:T(8,128)(2,1)}, u32[]{:S(2)}) copy-start(bf16[256,256]{1,0:T(8,128)(2,1)} %param.11) | copy-start | bytes 393220
  7.2 9.6 %copy-start.3 = (s32[1,1,2,256]{3,2,1,0:T(2,128)S(1)}, s32[1,1,2,256]{3,2,1,0:T(2,128)}, u32[]{:S(2)}) copy-start(s32[1,1,2,256]{3,2,1,0:T(2,128)} %param.14) | copy-start | bytes 6148
  9.7 38.2 %all-to-all-start = ((bf16[16,256,256]{2,1,0:T(8,128)(2,1)}), bf16[16,256,256]{2,1,0:T(8,128)(2,1)S(1)}, u32[]{:S(2)}, u32[]{:S(2)}) async-start(bf16[16,256,256]{2,1,0:T(8,128)(2,1)} %stack.2), calls=%async_computation | async-start | bytes 4194304 | tf_op jit(solution)/shard_map/all_to_all | solution.py:67
  16.7 183.6 %reduce-scatter.3.cloned.1.call-start = ((), (), s32[]{:S(2)}) async-start(), calls=%async_computation.3 | async-start | bytes 2228224 | tf_op jit(solution)/shard_map/reduce_scatter | solution.py:76
  143.6 56.8 %copy-start.4 = (bf16[256,256]{1,0:T(8,128)(2,1)S(1)}, bf16[256,256]{1,0:T(8,128)(2,1)}, u32[]{:S(2)}) copy-start(bf16[256,256]{1,0:T(8,128)(2,1)} %param.12) | copy-start | bytes 393220
  146.0 98.0 %all-gather.2.cloned.1.call-start = ((), (), s32[]{:S(2)}) async-start(), calls=%async_computation.5 | async-start | bytes 2228224 | tf_op jit(solution)/shard_map/all_gather | solution.py:85
  203.1 12.1 %copy-start.2 = (bf16[256,256]{1,0:T(8,128)(2,1)S(1)}, bf16[256,256]{1,0:T(8,128)(2,1)}, u32[]{:S(2)}) copy-start(bf16[256,256]{1,0:T(8,128)(2,1)} %reduce-scatter.3.cloned.1.call-done) | copy-start | bytes 393220
  203.1 294.0 %all-reduce.2.cloned.1.call-start = ((), (), s32[]{:S(2)}) async-start(), calls=%async_computation.4 | async-start | bytes 524288 | tf_op jit(solution)/shard_map/psum | solution.py:89
  216.1 368.0 %reduce-scatter.5.cloned.1.call-start = ((), (), s32[]{:S(2)}) async-start(), calls=%async_computation.6 | async-start | bytes 2228224 | tf_op jit(solution)/shard_map/reduce_scatter | solution.py:91
  343.7 240.4 %copy-start.1 = (bf16[256,256]{1,0:T(8,128)(2,1)S(1)}, bf16[256,256]{1,0:T(8,128)(2,1)}, u32[]{:S(2)}) copy-start(bf16[256,256]{1,0:T(8,128)(2,1)} %param.11) | copy-start | bytes 393220
Sparse Core Ops, SparseCore 0:
  146.1 54.2 reduce-scatter.2
  203.2 40.6 all-gather.1
  249.9 247.1 all-reduce.1
  500.1 83.9 reduce-scatter.4
